TPU v7x, 32 devices: a whole 2x2x4 slice. The times are simulated.
32 devices in a mesh: rows: 16 (over z, x, core), grp: 2 (over y).
Axes of the slice: x: 2, y: 2, z: 4, core: 2. Of those that a mesh axis runs over, the one named last changes fastest.
Arguments:
- snapshots: float32 [131072, 256], P(('rows', 'grp'))
- blocks: bfloat16 [1024, 16, 128, 128], P(('rows', 'grp')), may hold values from -48 to 48
- columns: int32 [1024, 16], P(('rows', 'grp')), may hold values from 0 to 63
Outputs:
- projected: float32 [256, 256], replicated
- scaled_factor: float32 [256, 256], replicated
Inputs may be any that keep to these rules, and one draw needn't show every extreme that they name: `columns`: each stored block couples its block row to a block row of the same group of 2 * 32 consecutive block rows.
All inputs are finite; a program needn't handle non-finite values.
Results may differ from a plain program's by a relative error of at most 0.003.
Values may be sent and summed in bfloat16 or wider, within the bound.
A program may use at most 192 MiB of HBM per device.

v0:
```python
import functools
import math

import jax
import jax.numpy as jnp
from jax import lax
from jax.experimental import pallas as pl
from jax.experimental.pallas import tpu as pltpu
from jax.sharding import PartitionSpec as P

HIGHEST = lax.Precision.HIGHEST
LANES = 128
SUB = 8
MESH = pl.DeviceIdType.MESH


def dot(left, right, dims=((1,), (0,)), precision=HIGHEST):
    return lax.dot_general(
        left, right, (dims, ((), ())), precision=precision, preferred_element_type=jnp.float32
    )


def across(value, lane, shape):
    return jnp.broadcast_to(value[..., lane : lane + 1], shape)


def eliminate(head, tail):
    tiles = head.shape[0]
    one = (SUB, LANES)
    for tile in range(tiles):
        base = tile * SUB
        rows_h = [jnp.broadcast_to(head[tile, k : k + 1, :], one) for k in range(SUB)]
        rows_t = [jnp.broadcast_to(tail[tile, k : k + 1, :], one) for k in range(SUB)]
        d = {}
        for k in range(SUB):
            for i in range(k, SUB):
                d[k, i] = across(rows_h[k], base + i, one)
        later = tiles - tile - 1
        if later:
            rest_h = head[tile + 1 :]
            rest_t = tail[tile + 1 :]
            low = [across(rest_h, base + k, (later, SUB, LANES)) for k in range(SUB)]
        for k in range(SUB):
            scale = lax.rsqrt(d[k, k])
            for i in range(k + 1, SUB):
                d[k, i] = d[k, i] * scale
            rows_h[k] = rows_h[k] * scale
            rows_t[k] = rows_t[k] * scale
            for i in range(k + 1, SUB):
                for m in range(i, SUB):
                    d[i, m] = d[i, m] - d[k, i] * d[k, m]
                rows_h[i] = rows_h[i] - d[k, i] * rows_h[k]
                rows_t[i] = rows_t[i] - d[k, i] * rows_t[k]
            if later:
                low[k] = low[k] * scale[None]
                for m in range(k + 1, SUB):
                    low[m] = low[m] - low[k] * d[k, m][None]
                rest_h = rest_h - low[k] * rows_h[k][None]
                rest_t = rest_t - low[k] * rows_t[k][None]
            head[tile, k : k + 1, :] = rows_h[k][:1]
            tail[tile, k : k + 1, :] = rows_t[k][:1]
        if later:
            head[tile + 1 :] = rest_h
            tail[tile + 1 :] = rest_t


def factor_kernel(gram_ref, factor_ref, inverse_ref, head, tail):
    size = gram_ref.shape[0]
    n = LANES
    row = lax.broadcasted_iota(jnp.int32, (n, n), 0)
    col = lax.broadcasted_iota(jnp.int32, (n, n), 1)
    eye = jnp.where(row == col, 1.0, 0.0).astype(jnp.float32)
    tiles = (n // SUB, SUB, n)
    count = size // n

    for b in range(count):
        here = slice(b * n, (b + 1) * n)
        square = gram_ref[here, here]
        for a in range(b):
            above = factor_ref[a * n : (a + 1) * n, here]
            square = square - dot(above, above, ((0,), (0,)))
        head[...] = square.reshape(tiles)
        tail[...] = eye.reshape(tiles)
        eliminate(head, tail)
        lower = jnp.where(row >= col, tail[...].reshape(n, n), 0.0)
        factor_ref[here, here] = jnp.where(row <= col, head[...].reshape(n, n), 0.0)
        upper = lower.T
        inverse_ref[here, here] = upper
        for c in range(b + 1, count):
            there = slice(c * n, (c + 1) * n)
            rest = gram_ref[here, there]
            for a in range(b):
                span = slice(a * n, (a + 1) * n)
                rest = rest - dot(factor_ref[span, here], factor_ref[span, there], ((0,), (0,)))
            factor_ref[here, there] = dot(lower, rest)
            factor_ref[there, here] = jnp.zeros((n, n), jnp.float32)
            inverse_ref[there, here] = jnp.zeros((n, n), jnp.float32)
        for a in range(b):
            span = slice(a * n, (a + 1) * n)
            total = jnp.zeros((n, n), jnp.float32)
            for m in range(a, b):
                mid = slice(m * n, (m + 1) * n)
                total = total + dot(inverse_ref[span, mid], factor_ref[mid, here])
            inverse_ref[span, here] = -dot(total, upper)


def factorize(gram):
    size = gram.shape[0]
    square = jax.ShapeDtypeStruct((size, size), jnp.float32)
    return pl.pallas_call(
        factor_kernel,
        out_shape=(square, square),
        in_specs=[pl.BlockSpec(memory_space=pltpu.VMEM)],
        out_specs=(pl.BlockSpec(memory_space=pltpu.VMEM),) * 2,
        scratch_shapes=[pltpu.VMEM((LANES // SUB, SUB, LANES), jnp.float32)] * 2,
        compiler_params=pltpu.CompilerParams(vmem_limit_bytes=16 * 2**20),
        name="factorize",
    )(gram)


def split(value):
    high = value.astype(jnp.bfloat16)
    return high, (value - high.astype(jnp.float32)).astype(jnp.bfloat16)


def mate_of(axes):
    row = lax.axis_index(axes[0])
    return {axes[0]: row + 1 - 2 * lax.rem(row, 2), axes[1]: lax.axis_index(axes[1])}


def greet(barrier, where):
    pl.semaphore_signal(barrier, inc=1, device_id=where, device_id_type=MESH)


def exchange(source, target, sems, where):
    return pltpu.make_async_remote_copy(
        src_ref=source, dst_ref=target, send_sem=sems.at[0], recv_sem=sems.at[1],
        device_id=where, device_id_type=MESH)


def near_kernel(axes, grps, x_ref, out_ref, pair, own, others, pair_sems, grp_sems):
    me_row, me_grp = lax.axis_index(axes[0]), lax.axis_index(axes[1])
    core = lax.rem(me_row, 2)
    mate = mate_of(axes)
    friends = [{axes[0]: me_row, axes[1]: lax.rem(me_grp + shift, grps)} for shift in range(1, grps)]
    barrier = pltpu.get_barrier_semaphore()
    for where in [mate] + friends:
        greet(barrier, where)
    pl.semaphore_wait(barrier, grps)
    first = exchange(x_ref.at[1 - core], pair, pair_sems, mate)
    first.start()
    first.wait()
    own[...] = x_ref[core] + pair[...]
    copies = [exchange(own, others.at[i], grp_sems.at[i], where) for i, where in enumerate(friends)]
    for copy in copies:
        copy.start()
    total = own[...]
    for i, copy in enumerate(copies):
        copy.wait()
        total = total + others[i]
    out_ref[...] = total


def near_sum(value, axes, chips):
    height, width = value.shape
    grps = lax.axis_size(axes[1])
    half = (chips, height // (2 * chips), width)
    f32 = jnp.float32
    return pl.pallas_call(
        functools.partial(near_kernel, axes, grps),
        out_shape=jax.ShapeDtypeStruct(half, f32),
        in_specs=[pl.BlockSpec(memory_space=pltpu.VMEM)],
        out_specs=pl.BlockSpec(memory_space=pltpu.VMEM),
        scratch_shapes=[
            pltpu.VMEM(half, f32),
            pltpu.VMEM(half, f32),
            pltpu.VMEM((grps - 1,) + half, f32),
            pltpu.SemaphoreType.DMA((2,)),
            pltpu.SemaphoreType.DMA((grps - 1, 2)),
        ],
        compiler_params=pltpu.CompilerParams(collective_id=1, has_side_effects=True),
        name="near_sum",
    )(value.reshape((2,) + half))


def sum_kernel(axes, grps, x_ref, out_ref, pair, own, slots, held, pair_sems, scatter_sems, gather_sems, last_sems):
    rows_axis, grp_axis = axes
    chips = own.shape[0]
    me_row, me_grp = lax.axis_index(rows_axis), lax.axis_index(grp_axis)
    core = lax.rem(me_row, 2)
    mate = mate_of(axes)
    whole = grps > 1
    me = (me_row // 2) * grps + me_grp if whole else me_row // 2

    def chip(offset):
        other = lax.rem(me + offset, chips)
        if whole:
            return other, {rows_axis: (other // grps) * 2 + core, grp_axis: lax.rem(other, grps)}
        return other, {rows_axis: other * 2 + core, grp_axis: me_grp}

    barrier = pltpu.get_barrier_semaphore()
    greet(barrier, mate)

    def greet_chip(offset, carry):
        greet(barrier, chip(offset)[1])
        return carry

    lax.fori_loop(1, chips, greet_chip, 0, unroll=chips <= 16)
    pl.semaphore_wait(barrier, chips)

    if whole:
        first = exchange(x_ref.at[1 - core], pair, pair_sems, mate)
        first.start()
        first.wait()
        own[...] = x_ref[core] + pair[...]
    else:
        own[...] = x_ref[...]

    def scatter(offset):
        other, where = chip(offset)
        return pltpu.make_async_remote_copy(
            src_ref=own.at[other], dst_ref=slots.at[offset],
            send_sem=scatter_sems.at[0, offset], recv_sem=scatter_sems.at[1, offset],
            device_id=where, device_id_type=MESH)

    def gather(offset):
        _, where = chip(offset)
        return pltpu.make_async_remote_copy(
            src_ref=held.at[core, me], dst_ref=held.at[core, me],
            send_sem=gather_sems.at[0, offset], recv_sem=gather_sems.at[1, offset],
            device_id=where, device_id_type=MESH)

    def each(make, act):
        def body(offset, carry):
            getattr(make(offset), act)()
            return carry
        lax.fori_loop(1, chips, body, 0, unroll=chips <= 16)

    each(scatter, "start")
    slots[0] = own[me]
    each(scatter, "wait_recv")
    held[core, me] = jnp.sum(slots[...], axis=0)
    each(gather, "start")
    each(scatter, "wait_send")
    each(gather, "wait_recv")
    last = exchange(held.at[core], held.at[core], last_sems, mate)
    last.start()
    each(gather, "wait_send")
    last.wait()
    out_ref[...] = held[...]


def device_sum(value, axes, whole=True):
    grps = lax.axis_size(axes[1]) if whole else 1
    chips = lax.axis_size(axes[0]) // 2 * grps
    height, width = (value.shape[0], value.shape[1]) if whole else (2 * chips * value.shape[1], value.shape[2])
    half = (chips, height // (2 * chips), width)
    f32 = jnp.float32
    out = pl.pallas_call(
        functools.partial(sum_kernel, axes, grps),
        out_shape=jax.ShapeDtypeStruct((2,) + half, f32),
        in_specs=[pl.BlockSpec(memory_space=pltpu.VMEM)],
        out_specs=pl.BlockSpec(memory_space=pltpu.VMEM),
        scratch_shapes=[
            pltpu.VMEM(half, f32),
            pltpu.VMEM(half, f32),
            pltpu.VMEM(half, f32),
            pltpu.VMEM((2,) + half, f32),
            pltpu.SemaphoreType.DMA((2,)),
            pltpu.SemaphoreType.DMA((2, chips)),
            pltpu.SemaphoreType.DMA((2, chips)),
            pltpu.SemaphoreType.DMA((2,)),
        ],
        compiler_params=pltpu.CompilerParams(collective_id=0 if whole else 2, has_side_effects=True),
        name="device_sum" if whole else "far_sum",
    )(value.reshape((2,) + half) if whole else value)
    return out.reshape(height, width)


def gram_kernel(early_tiles, *refs):
    *s_refs, out_ref, raw_ref, cross_ref = refs
    step = pl.program_id(0)
    value = jnp.concatenate([s_ref[...] for s_ref in s_refs], axis=0)
    high = value.astype(jnp.bfloat16)
    rest = value - high.astype(jnp.float32)
    mid = rest.astype(jnp.bfloat16)
    low = (rest - mid.astype(jnp.float32)).astype(jnp.bfloat16)
    rows = ((0,), (0,))
    square = dot(high, high, rows, None) + dot(mid, mid, rows, None)
    cross = dot(high, mid, rows, None) + dot(high, low, rows, None)

    @pl.when(step == 0)
    def _():
        out_ref[...] = square
        cross_ref[...] = cross

    @pl.when(step > 0)
    def _():
        out_ref[...] += square
        cross_ref[...] += cross

    @pl.when(step < early_tiles)
    def _():
        raw_ref[...] = value

    @pl.when(step == pl.num_programs(0) - 1)
    def _():
        cross = cross_ref[...]
        out_ref[...] += cross + cross.T


def gram_of(snapshots, early, tile=512, streams=4):
    height, width = snapshots.shape
    early_tiles = early // tile
    return pl.pallas_call(
        functools.partial(gram_kernel, early_tiles),
        grid=(height // tile,),
        in_specs=[
            pl.BlockSpec((tile // streams, width), functools.partial(lambda q, i: (i * streams + q, 0), q))
            for q in range(streams)
        ],
        out_specs=(
            pl.BlockSpec((width, width), lambda i: (0, 0)),
            pl.BlockSpec((tile, width), lambda i: (jnp.minimum(i, early_tiles - 1), 0)),
        ),
        out_shape=(
            jax.ShapeDtypeStruct((width, width), jnp.float32),
            jax.ShapeDtypeStruct((early, width), jnp.float32),
        ),
        scratch_shapes=[pltpu.VMEM((width, width), jnp.float32)],
        compiler_params=pltpu.CompilerParams(vmem_limit_bytes=60 * 2**20),
        name="gram",
    )(*[snapshots] * streams)


def split3(value):
    high = value.astype(jnp.bfloat16)
    rest = value - high.astype(jnp.float32)
    return (high,) + split(rest)


def basis_kernel(s_ref, inverse_ref, *outs):
    sh, sm, sl = split3(s_ref[...])
    wh, wm, wl = split3(inverse_ref[...])
    plain = ((1,), (0,))
    small = dot(sl, wh, plain, None) + dot(sm, wm, plain, None) + dot(sh, wl, plain, None)
    value = small + (dot(sm, wh, plain, None) + dot(sh, wm, plain, None)) + dot(sh, wh, plain, None)
    for out in outs:
        out[...] = value.astype(out.dtype)


def basis_of(rows, inverse, start, stop, dtypes, limit=16, tile=512):
    width = rows.shape[1]
    first = start // tile
    spec = pl.BlockSpec((tile, width), lambda i: (i, 0))
    return pl.pallas_call(
        basis_kernel,
        grid=((stop - start) // tile,),
        in_specs=[
            pl.BlockSpec((tile, width), lambda i: (i + first, 0)),
            pl.BlockSpec((width, width), lambda i: (0, 0)),
        ],
        out_specs=tuple(spec for _ in dtypes),
        out_shape=tuple(jax.ShapeDtypeStruct((stop - start, width), dtype) for dtype in dtypes),
        compiler_params=pltpu.CompilerParams(vmem_limit_bytes=limit * 2**20),
        cost_estimate=pl.CostEstimate(
            flops=12 * (stop - start) * width * width,
            bytes_accessed=8 * (stop - start) * width, transcendentals=0),
        name="basis",
    )(rows, inverse)


def fill(window_ref, sems, parts, block_len):
    copies, at = [], 0
    for index, part in enumerate(parts):
        size = part.shape[0]
        copies.append(pltpu.make_async_copy(part, window_ref.at[pl.ds(at, size)], sems.at[index]))
        at += size
    for copy in copies:
        copy.start()
    window_ref[at : at + block_len] = jnp.zeros((block_len, window_ref.shape[1]), window_ref.dtype)
    for copy in copies:
        copy.wait()


def project_kernel(per_step, slots, edges, n_parts, *refs):
    places_ref, picks_ref, counts_ref = refs[:3]
    block_refs, refs = refs[3 : 3 + per_step], refs[3 + per_step :]
    basis_refs = refs[: len(edges)]
    before_ref = refs[len(edges)]
    parts = refs[1 + len(edges) : 1 + len(edges) + n_parts]
    out_ref, window_ref, image_ref, sems = refs[1 + len(edges) + n_parts :]
    step = pl.program_id(0)
    stored, block_len = block_refs[0].shape[1], block_refs[0].shape[2]

    @pl.when(step == 0)
    def _():
        out_ref[...] = before_ref[...]
        fill(window_ref, sems, parts, block_len)

    def product(r, first):
        row = step * per_step + r
        lefts, rights = [], []
        for slot in range(first, first + slots):
            at = places_ref[row, slot] * block_len
            rights.append(window_ref[pl.ds(pl.multiple_of(at, block_len), block_len), :])
            lefts.append(block_refs[r][0, slot if slots == stored else picks_ref[row, slot]])
        left = jnp.concatenate(lefts, axis=1)
        right = jnp.concatenate(rights, axis=0)
        return jnp.dot(left, right, preferred_element_type=jnp.float32)

    for r in range(per_step):
        image_ref[r * block_len : (r + 1) * block_len] = product(r, 0)
    for first in range(slots, stored, slots):
        for r in range(per_step):

            @pl.when(counts_ref[step * per_step + r, 0] > first)
            def _():
                image_ref[r * block_len : (r + 1) * block_len] += product(r, first)

    value = basis_refs[-1][...]
    for edge, ref in reversed(list(zip(edges[1:], basis_refs[:-1]))):
        value = jnp.where(step < edge, ref[...], value)
    image_high, image_low = split(image_ref[...])
    basis_high, basis_low = split(value)
    rows = ((0,), (0,))
    term = dot(basis_high, image_high, rows, None)
    term = term + dot(basis_high, image_low, rows, None)
    term = term + dot(basis_low, image_high, rows, None)
    out_ref[...] += term


def project(places, picks, counts, blocks, basis, before, parts, slots, per_step=4):
    block_rows, stored, block_len, _ = blocks.shape
    width = before.shape[1]
    depth = sum(part.shape[0] for part in parts) + block_len
    tall = per_step * block_len
    edges, specs, at = [], [], 0
    for part in basis:
        steps = part.shape[0] // tall
        edges.append(at)
        specs.append(pl.BlockSpec(
            (tall, width),
            functools.partial(lambda at, steps, i, *_: (jnp.clip(i - at, 0, steps - 1), 0), at, steps)))
        at += steps
    grid_spec = pltpu.PrefetchScalarGridSpec(
        num_scalar_prefetch=3,
        grid=(block_rows // per_step,),
        in_specs=[
            pl.BlockSpec(
                (1, stored, block_len, block_len),
                functools.partial(lambda r, i, *_: (i * per_step + r, 0, 0, 0), r))
            for r in range(per_step)
        ]
        + specs
        + [pl.BlockSpec((width, width), lambda i, *_: (0, 0))]
        + [pl.BlockSpec(memory_space=pl.ANY)] * len(parts),
        out_specs=pl.BlockSpec((width, width), lambda i, *_: (0, 0)),
        scratch_shapes=[
            pltpu.VMEM((depth, width), jnp.bfloat16),
            pltpu.VMEM((tall, width), jnp.float32),
            pltpu.SemaphoreType.DMA((len(parts),)),
        ],
    )
    return pl.pallas_call(
        functools.partial(project_kernel, per_step, slots, tuple(edges), len(parts)),
        grid_spec=grid_spec,
        out_shape=jax.ShapeDtypeStruct((width, width), jnp.float32),
        compiler_params=pltpu.CompilerParams(vmem_limit_bytes=44 * 2**20),
        cost_estimate=pl.CostEstimate(
            flops=2 * block_rows * slots * block_len * block_len * width,
            bytes_accessed=blocks.size * 2, transcendentals=0),
        name="project",
    )(places, picks, counts, *[blocks] * per_step, *basis, before, *parts)


def ring(value, axis):
    size = lax.axis_size(axis)
    for shift in range(1, size):
        yield lax.ppermute(value, axis, [((d + shift) % size, d) for d in range(size)])


def plan_kernel(size, early, columns_ref, places_ref, picks_ref, late_places_ref, counts_ref):
    block_rows, stored = columns_ref.shape
    turned = lax.rem(columns_ref[...] + (size - lax.axis_index("grp")) * block_rows, size * block_rows)
    slab, row = turned // block_rows, lax.rem(turned, block_rows)
    wanted = jnp.where((slab == 0) | (row < early), 0, 1)
    near = jnp.where(slab == 0, row, block_rows + (slab - 1) * early + row)
    places_ref[...] = jnp.where(wanted == 1, block_rows + (size - 1) * early, near)
    late = (slab - 1) * (block_rows - early) + row - early
    slot = lax.broadcasted_iota(jnp.int32, (block_rows, stored), 1)
    rank = jnp.zeros((block_rows, stored), jnp.int32)
    picks = jnp.zeros((block_rows, stored), jnp.int32)
    late_places = jnp.full((block_rows, stored), (size - 1) * (block_rows - early), jnp.int32)
    for j in range(stored):
        needs = across(wanted, j, rank.shape)
        here = (needs == 1) & (rank == slot)
        picks = jnp.where(here, j, picks)
        late_places = jnp.where(here, across(late, j, rank.shape), late_places)
        rank = rank + needs
    picks_ref[...] = picks
    late_places_ref[...] = late_places
    counts_ref[...] = rank


def plan(columns, size, early):
    return pl.pallas_call(
        functools.partial(plan_kernel, size, early),
        out_shape=(jax.ShapeDtypeStruct(columns.shape, jnp.int32),) * 4,
        name="plan",
    )(columns)


def local(snapshots, blocks, columns):
    axes = ("rows", "grp")
    height, width = snapshots.shape
    block_len, stored = blocks.shape[2], blocks.shape[1]
    size = lax.axis_size("grp")
    early = height * 3 // 8
    half, full = jnp.bfloat16, jnp.float32
    places, picks, late_places, counts = plan(columns, size, early // block_len)
    gram, raw = gram_of(snapshots, early)
    near = near_sum(gram, axes, lax.axis_size("rows") // 2)
    near, raw = lax.optimization_barrier((near, raw))
    raws = list(ring(raw, "grp"))
    factor, inverse = factorize(device_sum(near, axes, whole=False))
    cuts = (early, height)
    pieces, halves, lates = [], [], []
    for start, stop in zip(cuts[:-1], cuts[1:]):
        piece, piece_half = basis_of(snapshots, inverse, start, stop, (full, half), 60)
        pieces.append(piece)
        halves.append(piece_half)
        lates.append(list(ring(piece_half, "grp")))
    piece, piece_half = basis_of(snapshots, inverse, 0, early, (full, half))
    basis = [piece] + pieces
    first = [piece_half] + halves + [basis_of(raw, inverse, 0, early, (half,))[0] for raw in raws]
    second = [late[index] for index in range(size - 1) for late in lates]
    zero = jnp.zeros((width, width), full)
    partial_terms = project(places, picks, counts, blocks, basis, zero, first, stored)
    partial_terms = project(late_places, picks, counts, blocks, basis, partial_terms, second, stored // 2)
    projected = device_sum(partial_terms, axes)
    total_rows = height * lax.axis_size(axes)
    return projected, factor / math.sqrt(total_rows)


def solution(mesh):
    return jax.shard_map(
        local,
        mesh=mesh,
        in_specs=(
            P(("rows", "grp"), None),
            P(("rows", "grp"), None, None, None),
            P(("rows", "grp"), None),
        ),
        out_specs=(P(), P()),
        check_vma=False,
    )
```

profile of v0, /device:TPU:0, one launch (start us, length us, event | category | flops | bytes accessed | tf_op | source)
XLA Modules:
  0.0 119.1 jit_solution(3180361553326055753)
XLA Ops:
  0.6 8.5 %gram.1 = (f32[256,256]{1,0:T(8,128)}, f32[1536,256]{1,0:T(8,128)}) custom-call(f32[4096,256]{1,0:T(8,128)} %s_ref.3, f32[4096,256]{1,0:T(8,128)} %s_ref.3, f32[4096,256]{1,0:T(8,128)} %s_ref.3, f32[4096,256]{1,0:T(8,128)} %s_ref.3), custom_call_target="tpu_custom_call" | custom-call | tf_op jit(solution)/shard_map/gram/pallas_call | solution.py:315
  9.2 9.8 %near_sum.1.x_ref = f32[8,16,256]{2,1,0:T(8,128)} custom-call(f32[2,8,16,256]{3,2,1,0:T(8,128)} %bitcast.7), custom_call_target="tpu_custom_call" | custom-call | tf_op jit(solution)/shard_map/near_sum/pallas_call | solution.py:169
  19.0 1.9 %collective-permute-start = (f32[1536,256]{1,0:T(8,128)}, f32[1536,256]{1,0:T(8,128)S(1)}, u32[]{:S(2)}, u32[]{:S(2)}) collective-permute-start(f32[1536,256]{1,0:T(8,128)} %get-tuple-element.28), channel_id=1, source_target_pairs={{1,0},{0,1},{3,2},{2,3},{5,4},{4,5},{7,6},{6,7},{9,8},{8,9},{11,10... | collective-permute-start | bytes 4718600 | tf_op jit(solution)/shard_map/ppermute | solution.py:480
  20.9 16.6 %far_sum.1 = f32[2,8,16,256]{3,2,1,0:T(8,128)} custom-call(f32[8,16,256]{2,1,0:T(8,128)} %near_sum.1.x_ref), custom_call_target="tpu_custom_call" | custom-call | tf_op jit(solution)/shard_map/far_sum/pallas_call | solution.py:259
  37.5 0.0 copy-start.4
  37.5 0.9 copy-done.4
  38.5 9.8 %factorize.1 = (f32[256,256]{1,0:T(8,128)S(1)}, f32[256,256]{1,0:T(8,128)S(1)}) custom-call(f32[256,256]{1,0:T(8,128)S(1)} %bitcast.5), custom_call_target="tpu_custom_call" | custom-call | tf_op jit(solution)/shard_map/factorize/pallas_call | solution.py:110
  48.3 0.0 copy-start.9
  48.3 0.7 copy-done.9
  49.0 6.5 %basis.4 = (f32[2560,256]{1,0:T(8,128)}, bf16[2560,256]{1,0:T(8,128)(2,1)}) custom-call(f32[4096,256]{1,0:T(8,128)} %s_ref.3, f32[256,256]{1,0:T(8,128)} %copy-done.9), custom_call_target="tpu_custom_call" | custom-call | flops 2013265920 | bytes 5242880 | tf_op jit(solution)/shard_map/basis/pallas_call | solution.py:356
  55.5 0.5 collective-permute-start.1
  56.0 0.0 copy-done.11
  56.0 0.7 copy.5.columns_ref
  56.7 1.6 %plan.1 = (s32[32,16]{1,0:T(8,128)}, s32[32,16]{1,0:T(8,128)}, s32[32,16]{1,0:T(8,128)}, s32[32,16]{1,0:T(8,128)}) custom-call(s32[32,16]{1,0:T(8,128)} %copy.5.columns_ref), custom_call_target="tpu_custom_call" | custom-call | tf_op jit(solution)/shard_map/plan/pallas_call | solution.py:507
  58.3 0.0 copy-done.10
  58.3 2.2 %copy-done = f32[4096,256]{1,0:T(8,128)S(1)} copy-done((f32[4096,256]{1,0:T(8,128)S(1)}, f32[4096,256]{1,0:T(8,128)}, u32[]{:S(2)}) %copy-start) | copy-done | bytes 4194328
  60.4 1.8 %basis.3 = (f32[1536,256]{1,0:T(8,128)S(1)}, bf16[1536,256]{1,0:T(8,128)(2,1)S(1)}) custom-call(f32[4096,256]{1,0:T(8,128)S(1)} %copy-done, f32[256,256]{1,0:T(8,128)S(1)} %copy-done.10), custom_call_target="tpu_custom_call" | custom-call | flops 1207959552 | bytes 3145728 | tf_op jit(solution)/shard_map/basis/pallas_call | solution.py:356
  62.3 0.7 broadcast_multiply_fusion
  63.0 0.0 copy-start.8
  63.0 0.0 collective-permute-done.s_ref
  63.0 1.8 %basis.5.refs_12_ = bf16[1536,256]{1,0:T(8,128)(2,1)S(1)} custom-call(f32[1536,256]{1,0:T(8,128)S(1)} %collective-permute-done.s_ref, f32[256,256]{1,0:T(8,128)S(1)} %copy-done.10), custom_call_target="tpu_custom_call" | custom-call | flops 1207959552 | bytes 3145728 | tf_op jit(solution)/shard_map/basis/pallas_call | solution.py:356
  64.9 0.0 copy-done.1
  64.9 0.2 copy-done.2
  65.1 0.0 copy-done.5
  65.1 0.0 copy-done.6
  65.1 13.5 %project.2.refs_9_ = f32[256,256]{1,0:T(8,128)S(1)} custom-call(s32[32,16]{1,0:T(8,128)S(1)} %copy-done.8, s32[32,16]{1,0:T(8,128)S(1)} %copy-done.5, s32[32,16]{1,0:T(8,128)S(1)} %copy-done.6, bf16[32,16,128,128]{3,2,1,0:T(8,128)(2,1)} %refs_6_.3, bf16[32,16,128,128]{3,2,1,0:T(8,128)(2,1)} %refs_6_.3, bf16[32,16,128,128]{3,2,1,0:T(8,128)(2,1)} %refs_6_.3, ...), custom_call_target="tpu_custom_call" | custom-call | flops 4294967296 | bytes 16777216 | tf_op jit(solution)/shard_map/project/pallas_call | solution.py:465
  78.7 8.1 %collective-permute-done.1.refs_10_ = bf16[2560,256]{1,0:T(8,128)(2,1)S(1)} collective-permute-done((bf16[2560,256]{1,0:T(8,128)(2,1)}, bf16[2560,256]{1,0:T(8,128)(2,1)S(1)}, u32[]{:S(2)}, u32[]{:S(2)}) %collective-permute-start.1) | collective-permute-done | bytes 1310752 | tf_op jit(solution)/shard_map/ppermute | solution.py:480
  86.8 12.5 %project.3 = f32[256,256]{1,0:T(8,128)S(1)} custom-call(s32[32,16]{1,0:T(8,128)S(1)} %copy-done.7, s32[32,16]{1,0:T(8,128)S(1)} %copy-done.5, s32[32,16]{1,0:T(8,128)S(1)} %copy-done.6, bf16[32,16,128,128]{3,2,1,0:T(8,128)(2,1)} %refs_6_.3, bf16[32,16,128,128]{3,2,1,0:T(8,128)(2,1)} %refs_6_.3, bf16[32,16,128,128]{3,2,1,0:T(8,128)(2,1)} %refs_6_.3, ...), custom_call_target="tpu_custom_call" | custom-call | flops 2147483648 | bytes 16777216 | tf_op jit(solution)/shard_map/project/pallas_call | solution.py:465
  99.3 0.0 copy-start.3
  99.3 0.7 copy-done.3
  100.0 17.4 %device_sum.1 = f32[2,16,8,256]{3,2,1,0:T(8,128)} custom-call(f32[2,16,8,256]{3,2,1,0:T(8,128)} %bitcast.4), custom_call_target="tpu_custom_call" | custom-call | tf_op jit(solution)/shard_map/device_sum/pallas_call | solution.py:259
  117.4 1.7 %copy.7 = f32[256,256]{1,0:T(8,128)} copy(f32[256,256]{1,0:T(8,128)} %bitcast.6) | data formatting | bytes 524288
  (11 shorter events, 0.0 us)
Async XLA Ops:
  19.0 44.1 %collective-permute-start = (f32[1536,256]{1,0:T(8,128)}, f32[1536,256]{1,0:T(8,128)S(1)}, u32[]{:S(2)}, u32[]{:S(2)}) collective-permute-start(f32[1536,256]{1,0:T(8,128)} %get-tuple-element.28), channel_id=1, source_target_pairs={{1,0},{0,1},{3,2},{2,3},{5,4},{4,5},{7,6},{6,7},{9,8},{8,9},{11,10... | collective-permute-start | bytes 4718600 | tf_op jit(solution)/shard_map/ppermute | solution.py:480
  37.5 1.0 copy-start.4
  48.3 0.7 copy-start.9
  49.0 7.0 %copy-start.11 = (s32[32,16]{0,1:T(8,128)S(1)}, s32[32,16]{0,1:T(8,128)}, u32[]{:S(2)}) copy-start(s32[32,16]{0,1:T(8,128)} %param.5) | copy-start | bytes 6148
  49.0 9.3 %copy-start.10 = (f32[256,256]{1,0:T(8,128)S(1)}, f32[256,256]{1,0:T(8,128)}, u32[]{:S(2)}) copy-start(f32[256,256]{1,0:T(8,128)} %copy-done.9) | copy-start | bytes 786436
  55.5 31.3 %collective-permute-start.1 = (bf16[2560,256]{1,0:T(8,128)(2,1)}, bf16[2560,256]{1,0:T(8,128)(2,1)S(1)}, u32[]{:S(2)}, u32[]{:S(2)}) collective-permute-start(bf16[2560,256]{1,0:T(8,128)(2,1)} %get-tuple-element.27.refs_11_), channel_id=1, source_target_pairs={{1,0},{0,1},{3,2},{2,3},{5,4},{4,5},{7,6},{6,7},{9,8},{8,9},{11,10... | collective-permute-start | bytes 3932168 | tf_op jit(solution)/shard_map/ppermute | solution.py:480
  58.3 2.2 %copy-start = (f32[4096,256]{1,0:T(8,128)S(1)}, f32[4096,256]{1,0:T(8,128)}, u32[]{:S(2)}) copy-start(f32[4096,256]{1,0:T(8,128)} %s_ref.3) | copy-start | bytes 12582916
  63.0 1.9 %copy-start.1 = (f32[2560,256]{1,0:T(8,128)S(1)}, f32[2560,256]{1,0:T(8,128)}, u32[]{:S(2)}) copy-start(f32[2560,256]{1,0:T(8,128)} %get-tuple-element.24.refs_8_) | copy-start | bytes 7864324
  63.0 2.1 %copy-start.2 = (bf16[2560,256]{1,0:T(8,128)(2,1)S(1)}, bf16[2560,256]{1,0:T(8,128)(2,1)}, u32[]{:S(2)}) copy-start(bf16[2560,256]{1,0:T(8,128)(2,1)} %get-tuple-element.27.refs_11_) | copy-start | bytes 3932164
  63.0 2.1 %copy-start.5 = (s32[32,16]{1,0:T(8,128)S(1)}, s32[32,16]{1,0:T(8,128)}, u32[]{:S(2)}) copy-start(s32[32,16]{1,0:T(8,128)} %get-tuple-element.17.refs_1_) | copy-start | bytes 6148
  63.0 2.1 %copy-start.6 = (s32[32,16]{1,0:T(8,128)S(1)}, s32[32,16]{1,0:T(8,128)}, u32[]{:S(2)}) copy-start(s32[32,16]{1,0:T(8,128)} %get-tuple-element.18.refs_2_) | copy-start | bytes 6148
  63.0 2.1 %copy-start.8 = (s32[32,16]{1,0:T(8,128)S(1)}, s32[32,16]{1,0:T(8,128)}, u32[]{:S(2)}) copy-start(s32[32,16]{1,0:T(8,128)} %get-tuple-element.25.refs_0_) | copy-start | bytes 6148
  65.1 21.7 %copy-start.7 = (s32[32,16]{1,0:T(8,128)S(1)}, s32[32,16]{1,0:T(8,128)}, u32[]{:S(2)}) copy-start(s32[32,16]{1,0:T(8,128)} %get-tuple-element.16.refs_0_) | copy-start | bytes 6148
  99.3 0.7 copy-start.3
where the time goes:
time: 120 us; the launch traced here: 119 us
  Pallas kernels  99.9 us (83%)
  waiting for transfers between devices  8.09 us (7%)
  local copies, waits for them, and re-layouts  7.15 us (6%)
  starting transfers between devices  2.44 us (2%)
    pallas_call x2, Pallas kernels, device_sum(): pl.pallas_call(functools.partial(sum_kernel, axes, grps), out_shape=jax.S...  34 us
    pallas_call x2, Pallas kernels, project(): pl.pallas_call(functools.partial(project_kernel, per_step, slots, tuple(e...  26.1 us
    pallas_call x3, Pallas kernels, basis_of(): pl.pallas_call(basis_kernel, grid=((stop - start) // tile,), in_specs=[pl...  10.1 us
    pallas_call x1, Pallas kernels, near_sum(): pl.pallas_call(functools.partial(near_kernel, axes, grps), out_shape=jax....  9.77 us
    pallas_call x1, Pallas kernels, factorize(): pl.pallas_call(factor_kernel, out_shape=(square, square), in_specs=[pl.Bl...  9.77 us
    pallas_call x1, Pallas kernels, gram_of(): pl.pallas_call(functools.partial(gram_kernel, early_tiles), grid=(height...  8.54 us
    ppermute x2, waiting for transfers between devices, ring(): lax.ppermute(value, axis, [((d + shift) % size, d) for d in range(size)])  8.09 us
    unnamed x26, local copies, waits for them, and re-layouts  7.13 us
  transfers between devices with their start and end apart: 2, of which 1 were waited for; matrix products, arithmetic and copies ran while one was open for 1% of the time, Pallas kernels for 43%

commit v1 on v0

--- a/solution.py
+++ b/solution.py
@@ -430,7 +430,7 @@
     out_ref[...] += term
 
 
-def project(places, picks, counts, blocks, basis, before, parts, slots, per_step=4):
+def project(places, picks, counts, blocks, basis, before, parts, slots, per_step=8):
     block_rows, stored, block_len, _ = blocks.shape
     width = before.shape[1]
     depth = sum(part.shape[0] for part in parts) + block_len
@@ -516,7 +516,7 @@
     height, width = snapshots.shape
     block_len, stored = blocks.shape[2], blocks.shape[1]
     size = lax.axis_size("grp")
-    early = height * 3 // 8
+    early = height // 2
     half, full = jnp.bfloat16, jnp.float32
     places, picks, late_places, counts = plan(columns, size, early // block_len)
     gram, raw = gram_of(snapshots, early)

time: 120 us -> 123 us (1.025)
  waiting for transfers between devices: 8.09 us -> 11.5 us
    pallas_call x2, Pallas kernels: 26.1 us -> 22.4 us  [project(): pl.pallas_call(functools.partial(project_kernel, per_step, slots, tuple(e...]
    ppermute x2, waiting for transfers between devices: 8.09 us -> 11.5 us  [ring(): lax.ppermute(value, axis, [((d + shift) % size, d) for d in range(size)])]
    pallas_call x2, Pallas kernels: 34 us -> 37.2 us  [device_sum(): pl.pallas_call(functools.partial(sum_kernel, axes, grps), out_shape=jax.S...]
  transfers between devices with their start and end apart: 2 -> 2, of which waited for: 1 -> 2; matrix products, arithmetic and copies ran while one was open for 1% -> 1% of each run, Pallas kernels for 43% -> 41%
where the time goes in v1:
time: 123 us
  Pallas kernels  99.5 us (81%)
  waiting for transfers between devices  11.5 us (9%)
  local copies, waits for them, and re-layouts  7.87 us (6%)
  starting transfers between devices  2.46 us (2%)
    pallas_call x2, Pallas kernels, device_sum(): pl.pallas_call(functools.partial(sum_kernel, axes, grps), out_shape=jax.S...  37.2 us
    pallas_call x2, Pallas kernels, project(): pl.pallas_call(functools.partial(project_kernel, per_step, slots, tuple(e...  22.4 us
    ppermute x2, waiting for transfers between devices, ring(): lax.ppermute(value, axis, [((d + shift) % size, d) for d in range(size)])  11.5 us
    pallas_call x3, Pallas kernels, basis_of(): pl.pallas_call(basis_kernel, grid=((stop - start) // tile,), in_specs=[pl...  9.93 us
    pallas_call x1, Pallas kernels, near_sum(): pl.pallas_call(functools.partial(near_kernel, axes, grps), out_shape=jax....  9.78 us
    pallas_call x1, Pallas kernels, factorize(): pl.pallas_call(factor_kernel, out_shape=(square, square), in_specs=[pl.Bl...  9.77 us
    pallas_call x1, Pallas kernels, gram_of(): pl.pallas_call(functools.partial(gram_kernel, early_tiles), grid=(height...  8.72 us
    unnamed x26, local copies, waits for them, and re-layouts  7.85 us
  transfers between devices with their start and end apart: 2, of which 2 were waited for; matrix products, arithmetic and copies ran while one was open for 1% of the time, Pallas kernels for 41%

profile of v1, /device:TPU:0, one launch (start us, length us, event | category | flops | bytes accessed | tf_op | source)
XLA Modules:
  0.0 122.8 jit_solution(11197259634432697833)
XLA Ops:
  0.6 8.7 %gram.1 = (f32[256,256]{1,0:T(8,128)}, f32[2048,256]{1,0:T(8,128)}) custom-call(f32[4096,256]{1,0:T(8,128)} %s_ref.3, f32[4096,256]{1,0:T(8,128)} %s_ref.3, f32[4096,256]{1,0:T(8,128)} %s_ref.3, f32[4096,256]{1,0:T(8,128)} %s_ref.3), custom_call_target="tpu_custom_call" | custom-call | tf_op jit(solution)/shard_map/gram/pallas_call | solution.py:315
  9.3 9.8 %near_sum.1.x_ref = f32[8,16,256]{2,1,0:T(8,128)} custom-call(f32[2,8,16,256]{3,2,1,0:T(8,128)} %bitcast.7), custom_call_target="tpu_custom_call" | custom-call | tf_op jit(solution)/shard_map/near_sum/pallas_call | solution.py:169
  19.1 1.9 %collective-permute-start = (f32[2048,256]{1,0:T(8,128)}, f32[2048,256]{1,0:T(8,128)S(1)}, u32[]{:S(2)}, u32[]{:S(2)}) collective-permute-start(f32[2048,256]{1,0:T(8,128)} %get-tuple-element.28), channel_id=1, source_target_pairs={{1,0},{0,1},{3,2},{2,3},{5,4},{4,5},{7,6},{6,7},{9,8},{8,9},{11,10... | collective-permute-start | bytes 6291464 | tf_op jit(solution)/shard_map/ppermute | solution.py:480
  21.1 16.6 %far_sum.1 = f32[2,8,16,256]{3,2,1,0:T(8,128)} custom-call(f32[8,16,256]{2,1,0:T(8,128)} %near_sum.1.x_ref), custom_call_target="tpu_custom_call" | custom-call | tf_op jit(solution)/shard_map/far_sum/pallas_call | solution.py:259
  37.7 0.0 copy-start.4
  37.7 0.9 copy-done.4
  38.7 9.8 %factorize.1 = (f32[256,256]{1,0:T(8,128)S(1)}, f32[256,256]{1,0:T(8,128)S(1)}) custom-call(f32[256,256]{1,0:T(8,128)S(1)} %bitcast.5), custom_call_target="tpu_custom_call" | custom-call | tf_op jit(solution)/shard_map/factorize/pallas_call | solution.py:110
  48.4 0.0 copy-start.9
  48.5 0.7 copy-done.9
  49.2 5.2 %basis.4 = (f32[2048,256]{1,0:T(8,128)}, bf16[2048,256]{1,0:T(8,128)(2,1)}) custom-call(f32[4096,256]{1,0:T(8,128)} %s_ref.3, f32[256,256]{1,0:T(8,128)} %copy-done.9), custom_call_target="tpu_custom_call" | custom-call | flops 1610612736 | bytes 4194304 | tf_op jit(solution)/shard_map/basis/pallas_call | solution.py:356
  54.3 0.5 collective-permute-start.1
  54.8 0.0 copy-done.11
  54.9 0.7 copy.5.columns_ref
  55.5 1.6 %plan.1 = (s32[32,16]{1,0:T(8,128)}, s32[32,16]{1,0:T(8,128)}, s32[32,16]{1,0:T(8,128)}, s32[32,16]{1,0:T(8,128)}) custom-call(s32[32,16]{1,0:T(8,128)} %copy.5.columns_ref), custom_call_target="tpu_custom_call" | custom-call | tf_op jit(solution)/shard_map/plan/pallas_call | solution.py:507
  57.1 2.2 %copy-done = f32[4096,256]{1,0:T(8,128)S(1)} copy-done((f32[4096,256]{1,0:T(8,128)S(1)}, f32[4096,256]{1,0:T(8,128)}, u32[]{:S(2)}) %copy-start) | copy-done | bytes 4194328
  59.3 0.9 copy-done.10
  60.3 2.4 %basis.3 = (f32[2048,256]{1,0:T(8,128)S(1)}, bf16[2048,256]{1,0:T(8,128)(2,1)S(1)}) custom-call(f32[4096,256]{1,0:T(8,128)S(1)} %copy-done, f32[256,256]{1,0:T(8,128)S(1)} %copy-done.10), custom_call_target="tpu_custom_call" | custom-call | flops 1610612736 | bytes 4194304 | tf_op jit(solution)/shard_map/basis/pallas_call | solution.py:356
  62.7 0.7 broadcast_multiply_fusion
  63.4 0.0 copy-start.8
  63.4 4.5 %collective-permute-done.s_ref = f32[2048,256]{1,0:T(8,128)S(1)} collective-permute-done((f32[2048,256]{1,0:T(8,128)}, f32[2048,256]{1,0:T(8,128)S(1)}, u32[]{:S(2)}, u32[]{:S(2)}) %collective-permute-start) | collective-permute-done | bytes 2097184 | tf_op jit(solution)/shard_map/ppermute | solution.py:480
  67.9 2.4 %basis.5.refs_16_ = bf16[2048,256]{1,0:T(8,128)(2,1)S(1)} custom-call(f32[2048,256]{1,0:T(8,128)S(1)} %collective-permute-done.s_ref, f32[256,256]{1,0:T(8,128)S(1)} %copy-done.10), custom_call_target="tpu_custom_call" | custom-call | flops 1610612736 | bytes 4194304 | tf_op jit(solution)/shard_map/basis/pallas_call | solution.py:356
  70.3 0.0 copy-done.1
  70.3 0.0 copy-done.2
  70.4 0.0 copy-done.5
  70.4 0.0 copy-done.6
  70.4 12.0 %project.2.refs_13_ = f32[256,256]{1,0:T(8,128)S(1)} custom-call(s32[32,16]{1,0:T(8,128)S(1)} %copy-done.8, s32[32,16]{1,0:T(8,128)S(1)} %copy-done.5, s32[32,16]{1,0:T(8,128)S(1)} %copy-done.6, bf16[32,16,128,128]{3,2,1,0:T(8,128)(2,1)} %refs_10_.3, bf16[32,16,128,128]{3,2,1,0:T(8,128)(2,1)} %refs_10_.3, bf16[32,16,128,128]{3,2,1,0:T(8,128)(2,1)} %refs_10_.3, ...), custom_call_target="tpu_custom_call" | custom-call | flops 4294967296 | bytes 16777216 | tf_op jit(solution)/shard_map/project/pallas_call | solution.py:465
  82.4 7.0 %collective-permute-done.1.refs_14_ = bf16[2048,256]{1,0:T(8,128)(2,1)S(1)} collective-permute-done((bf16[2048,256]{1,0:T(8,128)(2,1)}, bf16[2048,256]{1,0:T(8,128)(2,1)S(1)}, u32[]{:S(2)}, u32[]{:S(2)}) %collective-permute-start.1) | collective-permute-done | bytes 1048608 | tf_op jit(solution)/shard_map/ppermute | solution.py:480
  89.3 10.5 %project.3 = f32[256,256]{1,0:T(8,128)S(1)} custom-call(s32[32,16]{1,0:T(8,128)S(1)} %copy-done.7, s32[32,16]{1,0:T(8,128)S(1)} %copy-done.5, s32[32,16]{1,0:T(8,128)S(1)} %copy-done.6, bf16[32,16,128,128]{3,2,1,0:T(8,128)(2,1)} %refs_10_.3, bf16[32,16,128,128]{3,2,1,0:T(8,128)(2,1)} %refs_10_.3, bf16[32,16,128,128]{3,2,1,0:T(8,128)(2,1)} %refs_10_.3, ...), custom_call_target="tpu_custom_call" | custom-call | flops 2147483648 | bytes 16777216 | tf_op jit(solution)/shard_map/project/pallas_call | solution.py:465
  99.8 0.0 copy-start.3
  99.8 0.7 copy-done.3
  100.5 20.6 %device_sum.1 = f32[2,16,8,256]{3,2,1,0:T(8,128)} custom-call(f32[2,16,8,256]{3,2,1,0:T(8,128)} %bitcast.4), custom_call_target="tpu_custom_call" | custom-call | tf_op jit(solution)/shard_map/device_sum/pallas_call | solution.py:259
  121.1 1.7 %copy.7 = f32[256,256]{1,0:T(8,128)} copy(f32[256,256]{1,0:T(8,128)} %bitcast.6) | data formatting | bytes 524288
  (11 shorter events, 0.0 us)
Async XLA Ops:
  19.1 48.8 %collective-permute-start = (f32[2048,256]{1,0:T(8,128)}, f32[2048,256]{1,0:T(8,128)S(1)}, u32[]{:S(2)}, u32[]{:S(2)}) collective-permute-start(f32[2048,256]{1,0:T(8,128)} %get-tuple-element.28), channel_id=1, source_target_pairs={{1,0},{0,1},{3,2},{2,3},{5,4},{4,5},{7,6},{6,7},{9,8},{8,9},{11,10... | collective-permute-start | bytes 6291464 | tf_op jit(solution)/shard_map/ppermute | solution.py:480
  37.7 1.0 copy-start.4
  48.4 0.7 copy-start.9
  49.2 5.7 %copy-start.11 = (s32[32,16]{0,1:T(8,128)S(1)}, s32[32,16]{0,1:T(8,128)}, u32[]{:S(2)}) copy-start(s32[32,16]{0,1:T(8,128)} %param.5) | copy-start | bytes 6148
  54.3 35.0 %collective-permute-start.1 = (bf16[2048,256]{1,0:T(8,128)(2,1)}, bf16[2048,256]{1,0:T(8,128)(2,1)S(1)}, u32[]{:S(2)}, u32[]{:S(2)}) collective-permute-start(bf16[2048,256]{1,0:T(8,128)(2,1)} %get-tuple-element.27.refs_15_), channel_id=1, source_target_pairs={{1,0},{0,1},{3,2},{2,3},{5,4},{4,5},{7,6},{6,7},{9,8},{8,9},{11,10... | collective-permute-start | bytes 3145736 | tf_op jit(solution)/shard_map/ppermute | solution.py:480
  57.1 2.2 %copy-start = (f32[4096,256]{1,0:T(8,128)S(1)}, f32[4096,256]{1,0:T(8,128)}, u32[]{:S(2)}) copy-start(f32[4096,256]{1,0:T(8,128)} %s_ref.3) | copy-start | bytes 12582916
  59.3 0.9 copy-start.10
  63.4 6.9 %copy-start.1 = (f32[2048,256]{1,0:T(8,128)S(1)}, f32[2048,256]{1,0:T(8,128)}, u32[]{:S(2)}) copy-start(f32[2048,256]{1,0:T(8,128)} %get-tuple-element.24.refs_12_) | copy-start | bytes 6291460
  63.4 6.9 %copy-start.2 = (bf16[2048,256]{1,0:T(8,128)(2,1)S(1)}, bf16[2048,256]{1,0:T(8,128)(2,1)}, u32[]{:S(2)}) copy-start(bf16[2048,256]{1,0:T(8,128)(2,1)} %get-tuple-element.27.refs_15_) | copy-start | bytes 3145732
  63.4 7.0 %copy-start.5 = (s32[32,16]{1,0:T(8,128)S(1)}, s32[32,16]{1,0:T(8,128)}, u32[]{:S(2)}) copy-start(s32[32,16]{1,0:T(8,128)} %get-tuple-element.17.refs_1_) | copy-start | bytes 6148
  63.4 7.0 %copy-start.6 = (s32[32,16]{1,0:T(8,128)S(1)}, s32[32,16]{1,0:T(8,128)}, u32[]{:S(2)}) copy-start(s32[32,16]{1,0:T(8,128)} %get-tuple-element.18.refs_2_) | copy-start | bytes 6148
  63.4 7.0 %copy-start.8 = (s32[32,16]{1,0:T(8,128)S(1)}, s32[32,16]{1,0:T(8,128)}, u32[]{:S(2)}) copy-start(s32[32,16]{1,0:T(8,128)} %get-tuple-element.25.refs_0_) | copy-start | bytes 6148
  70.4 19.0 %copy-start.7 = (s32[32,16]{1,0:T(8,128)S(1)}, s32[32,16]{1,0:T(8,128)}, u32[]{:S(2)}) copy-start(s32[32,16]{1,0:T(8,128)} %get-tuple-element.16.refs_0_) | copy-start | bytes 6148
  99.8 0.7 copy-start.3
